TPU v7x, 256 devices: a whole 4x4x8 slice. The times are simulated.
256 devices in a mesh: seq: 64 (over y, z, x_lo), chan: 4 (over x_hi, core).
Axes of the slice: x: 4 (x_hi: 2, x_lo: 2; x = x_hi * 2 + x_lo), y: 4, z: 8, core: 2. Of those that a mesh axis runs over, the one named last changes fastest.
Arguments:
- inputs: bfloat16 [2, 65536, 2048], P(None, 'seq', 'chan'), may hold values from -6 to 6
- mix_first: bfloat16 [256, 256, 256], P('seq'), may hold values from -0.375 to 0.375
- mix_second: bfloat16 [256, 256, 256], P('seq'), may hold values from -0.375 to 0.375
- gate_scale: float32 [2048], P('chan'), may hold values from 0.5 to 2
- gate_bias: float32 [2048], P('chan'), may hold values from -3 to 3
- up_first: bfloat16 [4, 512, 512], P('chan'), may hold values from -0.25 to 0.25
- up_second: bfloat16 [4, 2048, 512], P('chan'), may hold values from -0.25 to 0.25
- down_first: bfloat16 [4, 512, 2048], P('chan'), may hold values from -0.125 to 0.125
- down_second: bfloat16 [4, 512, 512], P('chan'), may hold values from -0.25 to 0.25
Outputs:
- layer_out: bfloat16 [2, 65536, 2048], P(None, ('seq', 'chan'))
All inputs are finite; a program needn't handle non-finite values.
Results may differ from a plain program's by a relative error of at most 0.008.
Values may be sent and summed in bfloat16 or wider, within the bound.
No kernel may reach another device: no remote copies, remote signals or barrier semaphores. Data moves between devices by JAX's collectives and lax.ppermute only.
A program may use at most 128 MiB of HBM per device.

v0:
```python
import functools

import jax
import jax.numpy as jnp
from jax import lax
from jax.experimental import pallas as pl
from jax.experimental.pallas import tpu as pltpu
from jax.sharding import PartitionSpec as P

BF16 = jnp.bfloat16
F32 = jnp.float32
BOTH = ("seq", "chan")
MIB = 1 << 20
FULL = 58
VMEM = pl.BlockSpec(memory_space=pltpu.VMEM)
HBM = pl.BlockSpec(memory_space=pltpu.HBM)
SMEM = pl.BlockSpec(memory_space=pltpu.SMEM)


def params(mib):
    return pltpu.CompilerParams(vmem_limit_bytes=mib * MIB)


def mm(a, b):
    return jnp.dot(a, b, preferred_element_type=F32)


def mm_nt(a, b):
    return lax.dot_general(a, b, (((1,), (1,)), ((), ())), preferred_element_type=F32)


def iota2(shape, axis):
    return lax.broadcasted_iota(jnp.int32, shape, axis)


def one_hot(shape, pick):
    return jnp.where(pick(iota2(shape, 0), iota2(shape, 1)), 1.0, 0.0).astype(BF16)


def first_kernel(x_hbm, m_hbm, o_ref, acc, x, m, sems):
    copies = []
    for a in range(4):
        copies.append(
            (
                pltpu.make_async_copy(m_hbm.at[a], m.at[a], sems.at[2 * a]),
                pltpu.make_async_copy(x_hbm.at[:, a], x.at[a], sems.at[2 * a + 1]),
            )
        )
    for pair in copies:
        for c in pair:
            c.start()
    for a in range(4):
        for c in copies[a]:
            c.wait()
        for s in range(2):
            acc[:, s * 4 + a, :] = mm(m[a], x[a, s])
    o_ref[...] = acc[...].reshape(64, 32, 512).astype(BF16)


def first_mix(x, m):
    return pl.pallas_call(
        first_kernel,
        out_shape=jax.ShapeDtypeStruct((64, 32, 512), BF16),
        in_specs=[HBM, HBM],
        out_specs=VMEM,
        scratch_shapes=[
            pltpu.VMEM((256, 8, 512), F32),
            pltpu.VMEM((4, 2, 256, 512), BF16),
            pltpu.VMEM((4, 256, 256), BF16),
            pltpu.SemaphoreType.DMA((8,)),
        ],
        compiler_params=params(FULL),
        cost_estimate=pl.CostEstimate(flops=2**29, bytes_accessed=5 * MIB, transcendentals=0),
        name="first_mix",
    )(x, m)


def spread_kernel(meta, m_ref, o_ref):
    rows = one_hot((256, 256), lambda r, x: x == (r % 64) * 4 + r // 64)
    for b in range(4):
        turned = mm(rows, m_ref[b]).astype(BF16)
        for s in range(2):
            slot = (b % 2) * 2 + s
            place = one_hot(
                (256, 1024),
                lambda y, k: k == (y // 4) * 16 + (b % 2) * 8 + s * 4 + y % 4,
            )
            o_ref[b // 2, slot * 256 : (slot + 1) * 256, :] = mm(turned, place).astype(BF16)


def spread(meta, m):
    return pl.pallas_call(
        spread_kernel,
        out_shape=jax.ShapeDtypeStruct((2, 1024, 1024), BF16),
        in_specs=[SMEM, VMEM],
        out_specs=VMEM,
        compiler_params=params(FULL),
        cost_estimate=pl.CostEstimate(flops=2**30, bytes_accessed=5 * MIB, transcendentals=0),
        name="spread",
    )(meta, m)


def second_kernel(r_hbm, m_hbm, o_ref, acc, r, m, sems):
    copies = []
    for p in range(2):
        rows = pl.ds(p * 16, 16)
        copies.append(pltpu.make_async_copy(r_hbm.at[:, rows, :], r.at[p], sems.at[2 * p]))
        copies.append(pltpu.make_async_copy(m_hbm.at[p], m.at[p], sems.at[2 * p + 1]))
    for c in copies:
        c.start()
    for p in range(2):
        copies[2 * p].wait()
        copies[2 * p + 1].wait()
        part = r[p].reshape(1024, 512)
        for slot in range(4):
            b, s = p * 2 + slot // 2, slot % 2
            acc[:, s * 4 + b, :] = mm(m[p, slot * 256 : (slot + 1) * 256, :], part)
    o_ref[...] = acc[...].astype(BF16)


def second_mix(received, m):
    return pl.pallas_call(
        second_kernel,
        out_shape=jax.ShapeDtypeStruct((256, 8, 512), BF16),
        in_specs=[HBM, HBM],
        out_specs=VMEM,
        scratch_shapes=[
            pltpu.VMEM((256, 8, 512), F32),
            pltpu.VMEM((2, 64, 16, 512), BF16),
            pltpu.VMEM((2, 1024, 1024), BF16),
            pltpu.SemaphoreType.DMA((4,)),
        ],
        compiler_params=params(34),
        cost_estimate=pl.CostEstimate(flops=2**31, bytes_accessed=8 * MIB, transcendentals=0),
        name="second_mix",
    )(received, m)


A_ROWS, B_ROWS = 656, 640


def same_rows(n, first):
    return one_hot((n, 512), lambda r, c: c == r + first)


def turned_rows(n, first):
    return one_hot((n, 512), lambda r, m: m == ((r + first) % 128) * 4 + (r + first) // 128)


def gate_rows(g_ref):
    rows = []
    for v in range(2):
        rest = g_ref[v : v + 1, :]
        for _ in range(3):
            part = rest.astype(BF16).astype(F32)
            rows.append(part)
            rest = rest - part
    return jnp.concatenate(rows + [jnp.zeros((10, 512), F32)], axis=0).astype(BF16)


def quarter_kernel(meta, g_ref, w1, w2, w3, w4, a_ref, b_ref, f_ref, v1, v2, v3, v5, v4, sem):
    y = meta[1]
    far = (y + 2) % 4
    near_at, far_at = pl.multiple_of(y * 512, 512), pl.multiple_of(far * 512, 512)
    copies = [
        pltpu.make_async_copy(w1.at[0], v1, sem.at[0]),
        pltpu.make_async_copy(w2.at[0, pl.ds(near_at, 512), :], v2, sem.at[1]),
        pltpu.make_async_copy(w3.at[0, :, pl.ds(near_at, 512)], v3, sem.at[2]),
        pltpu.make_async_copy(w3.at[0, :, pl.ds(far_at, 512)], v5, sem.at[3]),
        pltpu.make_async_copy(w4.at[0], v4, sem.at[4]),
    ]
    for c in copies:
        c.start()
    for c in copies:
        c.wait()
    a_ref[0:128, :] = mm_nt(same_rows(128, y * 128), v1[...]).astype(BF16)
    a_ref[128:640, :] = mm_nt(turned_rows(512, 0), v2[...]).astype(BF16)
    a_ref[640:656, :] = gate_rows(g_ref)
    for at, v, out in ((y, v3, b_ref), (far, v5, f_ref)):
        out[0:512, :] = mm_nt(same_rows(512, 0), v[...]).astype(BF16)
        out[512:640, :] = mm_nt(turned_rows(128, at * 128), v4[...]).astype(BF16)


def quarter(meta, gate, w1, w2, w3, w4):
    b_piece = jax.ShapeDtypeStruct((B_ROWS, 512), BF16)
    return pl.pallas_call(
        quarter_kernel,
        out_shape=(jax.ShapeDtypeStruct((A_ROWS, 512), BF16), b_piece, b_piece),
        in_specs=[SMEM, VMEM] + [HBM] * 4,
        out_specs=(VMEM, VMEM, VMEM),
        scratch_shapes=[pltpu.VMEM((512, 512), BF16)] * 5 + [pltpu.SemaphoreType.DMA((5,))],
        compiler_params=params(FULL),
        cost_estimate=pl.CostEstimate(flops=2**29, bytes_accessed=4 * MIB, transcendentals=0),
        name="quarter",
    )(meta, gate, w1, w2, w3, w4)


def pack_kernel(meta, g_ref, w1, w2, w3, w4, *o_refs):
    same = same_rows(512, 0)
    turn = turned_rows(512, 0)
    first = mm_nt(same, w1[0]).astype(BF16)
    last = mm_nt(turn, w4[0]).astype(BF16)
    for j in range(4):
        wide = slice(j * 512, (j + 1) * 512)
        o_refs[j][0:128, :] = first[j * 128 : (j + 1) * 128]
        o_refs[j][128:640, :] = mm_nt(turn, w2[0, wide, :]).astype(BF16)
        o_refs[j][640:656, :] = gate_rows(g_ref)
        o_refs[j][656:1168, :] = mm_nt(same, w3[0, :, wide]).astype(BF16)
        o_refs[j][1168:1296, :] = last[j * 128 : (j + 1) * 128]


def pack(meta, gate, w1, w2, w3, w4):
    return pl.pallas_call(
        pack_kernel,
        out_shape=(jax.ShapeDtypeStruct((A_ROWS + B_ROWS, 512), BF16),) * 4,
        in_specs=[SMEM] + [VMEM] * 5,
        out_specs=(VMEM,) * 4,
        compiler_params=params(FULL),
        cost_estimate=pl.CostEstimate(flops=2**31, bytes_accessed=10 * MIB, transcendentals=0),
        name="pack",
    )(meta, gate, w1, w2, w3, w4)


LOW = 320
PIECES = (
    (0, 656, 0),
    (0, 656, 3),
    (0, 656, 1),
    (0, LOW, 2),
    (LOW, 656, 2),
    (656, 1296, 0),
    (656, 1296, 3),
    (656, 1296, 1),
    (656, 1296, 2),
)
SPANS = ((0, 128), (128, 640), (640, 656), (656, 1168), (1168, 1296))


def mlp_kernel(
    meta, r_hbm, x0, x1, x2, x3, *refs
):
    own, swapped, refs = refs[:4], refs[4:8], refs[8:]
    pieces, refs = (refs[:9], refs[9:18]), refs[18:]
    o_hbm, act, out, rec, xin, gate, hid, mid, mid2, w1, w2, w3, w4, sems, o_sems = refs
    chan, y = meta[0], meta[1]
    waits = {}
    count = [0]

    def fetch(key, src, dst):
        copy = pltpu.make_async_copy(src, dst, sems.at[count[0]])
        count[0] += 1
        copy.start()
        waits.setdefault(key, []).append(copy)

    def fetch_part(part, k):
        dst = (w1, w2, gate, w3, w4)[part]
        lo, hi = SPANS[part]
        block = chan ^ k
        if k < 2:
            for j in range(1 if part == 2 else 4):
                to = dst.at[block] if part == 2 else dst.at[block, j]
                fetch((part, k), (own, swapped)[k][j].at[lo:hi, :], to)
        else:
            for src, (first, end, offset) in zip(pieces[k - 2], PIECES):
                a, b = max(lo, first), min(hi, end)
                if a >= b or (part == 2 and offset):
                    continue
                to = dst.at[block]
                if part != 2:
                    to = dst.at[block, (y + offset) % 4, a - lo : b - lo, :]
                fetch((part, k), src.at[a - first : b - first, :], to)

    def ready(part, k):
        for copy in waits[(part, k)]:
            copy.wait()

    def fetch_rows(k):
        fetch((5, k), r_hbm.at[chan ^ k], rec.at[k])
        fetch((5, k), (x0, x1, x2, x3)[k], xin.at[k])
        fetch_part(2, k)
        fetch_part(0, k)

    for k in range(4):
        fetch_rows(k)
    fetch_part(1, 0)
    fetch_part(3, 0)
    fetch_part(1, 1)
    fetch_part(3, 1)
    fetch_part(1, 2)
    fetch_part(3, 2)
    fetch_part(1, 3)
    fetch_part(3, 3)
    for n in range(4):
        fetch_part(4, n)
    order = one_hot(
        (512, 512),
        lambda r, k: k == ((r % 256) // 4) * 8 + (r // 256) * 4 + r % 4,
    )
    def first_stage(k, carry):
        @pl.when(k == 1)
        def _():
            for n in (1, 2, 3):
                ready(5, n)
                ready(2, n)
                ready(0, n)

        c = chan ^ k
        mixed = mm(order, rec[k])
        res = xin[k].reshape(512, 512).astype(F32)
        g = gate[c].astype(F32)
        scale = (g[0:1] + g[1:2]) + g[2:3]
        bias = (g[3:4] + g[4:5]) + g[5:6]
        z = scale * res + bias
        hidden = (res + mixed * (0.5 * jnp.tanh(0.5 * z) + 0.5)).astype(BF16)
        hid[c] = hidden
        inner = mm(hidden, w1[c].reshape(512, 512)).astype(BF16)
        for l in range(4):
            mid[l, c] = inner[:, l * 128 : (l + 1) * 128]
        return carry

    def second_stage(k, carry):
        @pl.when(k == 2)
        def _():
            for n in (2, 3):
                ready(1, n)
                ready(3, n)
            for n in range(4):
                ready(4, n)

        l = chan ^ k
        rows = jnp.concatenate([mid[l, c] for c in range(4)], axis=1)
        for j in range(4):
            e = mm(rows, w2[l, j])
            u = e * (0.7978845608028654 + 0.035677408136300125 * (e * e))
            half = 0.5 * e
            act[:, j * 512 : (j + 1) * 512] = (half + half * jnp.tanh(u)).astype(BF16)
        inner = mm(act[...], w3[l].reshape(2048, 512)).astype(BF16)
        for n in range(4):
            mid2[n, l] = inner[:, n * 128 : (n + 1) * 128]
        return carry

    for key in (5, 2, 0):
        ready(key, 0)
    lax.fori_loop(0, 4, first_stage, 0)
    for n in (0, 1):
        ready(1, n)
        ready(3, n)
    lax.fori_loop(0, 4, second_stage, 0)
    stores = []
    for k in range(4):
        n = chan ^ k
        rows = jnp.concatenate([mid2[n, l] for l in range(4)], axis=1)
        t = mm(rows, w4[n].reshape(512, 512))
        out[k] = (hid[n].astype(F32) + t).astype(BF16).reshape(2, 256, 512)
        lanes = pl.ds(pl.multiple_of(n * 512, 512), 512)
        stores.append(pltpu.make_async_copy(out.at[k], o_hbm.at[:, :, lanes], o_sems.at[k]))
        stores[k].start()
    for copy in stores:
        copy.wait()


def mlp(meta, received, xs, own, swapped, near, cross):
    wide = pltpu.VMEM((4, 4, 512, 512), BF16)
    narrow = pltpu.VMEM((4, 4, 128, 512), BF16)
    tall = pltpu.VMEM((4, 4, 512, 128), BF16)
    square = pltpu.VMEM((4, 512, 512), BF16)
    halves = pltpu.VMEM((4, 2, 256, 512), BF16)
    return pl.pallas_call(
        mlp_kernel,
        out_shape=jax.ShapeDtypeStruct((2, 256, 2048), BF16),
        in_specs=[SMEM] + [HBM] * 31,
        out_specs=HBM,
        scratch_shapes=[
            pltpu.VMEM((512, 2048), BF16),
            halves,
            square,
            halves,
            pltpu.VMEM((4, 16, 512), BF16),
            square,
            tall,
            tall,
            narrow,
            wide,
            wide,
            narrow,
            pltpu.SemaphoreType.DMA((80,)),
            pltpu.SemaphoreType.DMA((4,)),
        ],
        compiler_params=params(FULL),
        cost_estimate=pl.CostEstimate(
            flops=11 * 2**30, bytes_accessed=26 * MIB, transcendentals=5 * MIB
        ),
        name="mlp",
    )(meta, received, *xs, *own, *swapped, *near, *cross)


def place(y, z, xl, h, c):
    return (((y % 4) * 8 + z) * 2 + xl) * 4 + h * 2 + c


def pairs(move):
    out = []
    for i in range(256):
        seq, chan = divmod(i, 4)
        y, rest = divmod(seq, 16)
        z, xl = divmod(rest, 2)
        out.append((i, place(*move(y, z, xl, chan // 2, chan % 2))))
    return out


def next_along_x(y, z, xl, h, c):
    return y, z, 1 - xl, 1 - h, c


TO_X = pairs(next_along_x)
TO_CORE = pairs(lambda y, z, xl, h, c: (y, z, xl, h, 1 - c))
TO_CHAN = [
    pairs(lambda y, z, xl, h, c, k=k: (y, z, xl, h ^ (k >> 1), c ^ (k & 1))) for k in range(4)
]


def along_y(step):
    return pairs(lambda y, z, xl, h, c: (y + step, z, xl, h, c))


def on_device(
    inputs, mix_first, mix_second, gate_scale, gate_bias, up_first, up_second, down_first, down_second
):
    bar = lax.optimization_barrier
    chan = lax.axis_index("chan")
    y = lax.axis_index("seq") // 16
    meta = jnp.stack([chan, y]).astype(jnp.int32)
    gate = jnp.stack([gate_scale, gate_bias])
    grouped = inputs.reshape(2, 4, 256, 512)
    move = lambda piece, to: lax.ppermute(piece, BOTH, to)
    swap = lambda piece: lax.ppermute(piece, BOTH, TO_CORE)

    sent = first_mix(grouped, mix_first)
    received = lax.all_to_all(sent, "seq", split_axis=0, concat_axis=0, tiled=True)
    _, meta = bar((sent, meta))
    mine_a, mine_b, mine_far = quarter(meta, gate, up_first, up_second, down_first, down_second)
    _, meta = bar((mine_a, meta))
    near_a, near_b = move(mine_a, TO_X), move(mine_b, TO_X)
    _, mine_far = bar((near_b, mine_far))
    far_b = move(mine_far, TO_X)
    up_a, down_a = move(near_a, along_y(1)), move(near_a, along_y(-1))
    own = pack(meta, gate, up_first, up_second, down_first, down_second)
    spread_second = spread(meta, mix_second)
    received, spread_second, near_a, near_b, far_b, up_a, down_a, own, meta = bar(
        (received, spread_second, near_a, near_b, far_b, up_a, down_a, own, meta)
    )
    swapped, cross_far = [swap(piece) for piece in own], swap(far_b)
    turned = second_mix(received, spread_second)
    turned, swapped, cross_far, near_a, near_b, up_a, down_a, meta = bar(
        (turned, swapped, cross_far, near_a, near_b, up_a, down_a, meta)
    )
    back = lax.all_to_all(turned, ("chan", "seq"), split_axis=0, concat_axis=0, tiled=True)
    xs = []
    for k in range(4):
        part = lax.dynamic_index_in_dim(grouped, meta[0] ^ k, 1, keepdims=False)
        xs.append(move(part, TO_CHAN[k]) if k else part)
    up_b, down_b = move(near_b, along_y(1)), move(near_b, along_y(-1))
    low, high = move(up_a[:LOW], along_y(1)), move(down_a[LOW:], along_y(-1))
    xs, up_b, down_b, low, high, near_a, up_a, down_a = bar(
        (xs, up_b, down_b, low, high, near_a, up_a, down_a)
    )
    near = [near_a, up_a, down_a, low, high, near_b, up_b, down_b, far_b]
    cross = [swap(piece) for piece in near[:8]] + [cross_far]
    return mlp(meta, back.reshape(4, 512, 512), xs, own, swapped, near, cross)


def solution(mesh):
    return jax.shard_map(
        on_device,
        mesh=mesh,
        in_specs=(
            P(None, "seq", "chan"),
            P("seq", None, None),
            P("seq", None, None),
            P("chan"),
            P("chan"),
            P("chan", None, None),
            P("chan", None, None),
            P("chan", None, None),
            P("chan", None, None),
        ),
        out_specs=P(None, ("seq", "chan"), None),
        check_vma=False,
    )
```

profile of v0, /device:TPU:1, one launch (start us, length us, event | category | flops | bytes accessed | tf_op | source)
XLA Modules:
  0.0 174.9 jit_solution(2688821241115749194)
XLA Ops:
  0.0 4.6 %first_mix.1 = bf16[64,32,512]{2,1,0:T(8,128)(2,1)} custom-call(bf16[2,4,256,512]{3,2,1,0:T(8,128)(2,1)} %bitcast.16, bf16[4,256,256]{2,1,0:T(8,128)(2,1)} %m_hbm.1), custom_call_target="tpu_custom_call" | custom-call | flops 536870912 | bytes 5242880 | tf_op jit(solution)/shard_map/first_mix/pallas_call | solution.py:61
  4.6 13.6 %all-to-all-start = ((bf16[64,32,512]{2,1,0:T(8,128)(2,1)}), bf16[64,32,512]{2,1,0:T(8,128)(2,1)S(1)}, u32[]{:S(2)}, u32[]{:S(2)}) async-start(bf16[64,32,512]{2,1,0:T(8,128)(2,1)} %first_mix.1), calls=%async_computation | async-start | bytes 4194304 | tf_op jit(solution)/shard_map/all_to_all | solution.py:439
  19.5 5.0 %quarter.1 = (bf16[656,512]{1,0:T(8,128)(2,1)}, bf16[640,512]{1,0:T(8,128)(2,1)}, bf16[640,512]{1,0:T(8,128)(2,1)}) custom-call(s32[2]{0:T(128)} %pad_add_fusion.meta, f32[2,512]{1,0:T(2,128)} %pad_maximum_fusion.g_ref, bf16[1,512,512]{2,1,0:T(8,128)(2,1)} %w1.3, bf16[1,2048,512]{2,1,0:T(8,128)(2,1)} %w2.3, bf16[1,512,2048]{2,1,0:T(8,128)(2,1)} %w3.3, ...), custom_call_target="tpu_custom_call" | custom-call | flops 536870912 | bytes 4194304 | tf_op jit(solution)/shard_map/quarter/pallas_call | solution.py:186
  24.5 2.4 %collective-permute-start = (bf16[656,512]{1,0:T(8,128)(2,1)}, bf16[656,512]{1,0:T(8,128)(2,1)S(1)}, u32[]{:S(2)}, u32[]{:S(2)}) collective-permute-start(bf16[656,512]{1,0:T(8,128)(2,1)} %get-tuple-element.50), channel_id=1, source_target_pairs={{0,6},{1,7},{2,4},{3,5},{4,2},{5,3},{6,0},{7,1},{8,14},{9,15},{10,... | collective-permute-start | bytes 2015240 | tf_op jit(solution)/shard_map/ppermute | solution.py:435
  27.2 14.4 %collective-permute-done.refs_8_ = bf16[656,512]{1,0:T(8,128)(2,1)S(1)} collective-permute-done((bf16[656,512]{1,0:T(8,128)(2,1)}, bf16[656,512]{1,0:T(8,128)(2,1)S(1)}, u32[]{:S(2)}, u32[]{:S(2)}) %collective-permute-start) | collective-permute-done | bytes 671776 | tf_op jit(solution)/shard_map/ppermute | solution.py:435
  41.6 2.1 %collective-permute-start.4 = (bf16[656,512]{1,0:T(8,128)(2,1)S(1)}, bf16[656,512]{1,0:T(8,128)(2,1)S(1)}, u32[]{:S(2)}, u32[]{:S(2)}) collective-permute-start(bf16[656,512]{1,0:T(8,128)(2,1)S(1)} %collective-permute-done.refs_8_), channel_id=1, source_target_pairs={{0,192},{1,193},{2,194},{3,195},{4,196},{5,197},{6,198},{7,199},{8... | collective-permute-start | bytes 2015240 | tf_op jit(solution)/shard_map/ppermute | solution.py:435
  43.7 12.0 %collective-permute-done.1.refs_13_ = bf16[640,512]{1,0:T(8,128)(2,1)S(1)} collective-permute-done((bf16[640,512]{1,0:T(8,128)(2,1)}, bf16[640,512]{1,0:T(8,128)(2,1)S(1)}, u32[]{:S(2)}, u32[]{:S(2)}) %collective-permute-start.1) | collective-permute-done | bytes 655392 | tf_op jit(solution)/shard_map/ppermute | solution.py:435
  55.7 2.0 %collective-permute-start.2 = (bf16[640,512]{1,0:T(8,128)(2,1)}, bf16[640,512]{1,0:T(8,128)(2,1)S(1)}, u32[]{:S(2)}, u32[]{:S(2)}) collective-permute-start(bf16[640,512]{1,0:T(8,128)(2,1)} %get-tuple-element.54), channel_id=1, source_target_pairs={{0,6},{1,7},{2,4},{3,5},{4,2},{5,3},{6,0},{7,1},{8,14},{9,15},{10,... | collective-permute-start | bytes 1966088 | tf_op jit(solution)/shard_map/ppermute | solution.py:435
  57.7 5.0 %spread.1.m_hbm = bf16[2,1024,1024]{2,1,0:T(8,128)(2,1)} custom-call(s32[2]{0:T(128)} %pad_add_fusion.meta, bf16[4,256,256]{2,1,0:T(8,128)(2,1)} %m_ref.1), custom_call_target="tpu_custom_call" | custom-call | flops 1073741824 | bytes 5242880 | tf_op jit(solution)/shard_map/spread/pallas_call | solution.py:92
  62.8 7.6 %pack.1 = (bf16[1296,512]{1,0:T(8,128)(2,1)}, bf16[1296,512]{1,0:T(8,128)(2,1)}, bf16[1296,512]{1,0:T(8,128)(2,1)}, bf16[1296,512]{1,0:T(8,128)(2,1)}) custom-call(s32[2]{0:T(128)} %pad_add_fusion.meta, f32[2,512]{1,0:T(2,128)} %pad_maximum_fusion.g_ref, bf16[1,512,512]{2,1,0:T(8,128)(2,1)} %w1.3, bf16[1,2048,512]{2,1,0:T(8,128)(2,1)} %w2.3, ...), custom_call_target="tpu_custom_call" | custom-call | flops 2147483648 | bytes 10485760 | tf_op jit(solution)/shard_map/pack/pallas_call | solution.py:213
  70.4 1.3 collective-permute-done.2.refs_16_
  71.8 2.7 %collective-permute-start.5 = (bf16[1296,512]{1,0:T(8,128)(2,1)}, bf16[1296,512]{1,0:T(8,128)(2,1)}, u32[]{:S(2)}, u32[]{:S(2)}) collective-permute-start(bf16[1296,512]{1,0:T(8,128)(2,1)} %get-tuple-element.61.refs_0_), channel_id=1, source_target_pairs={{0,1},{1,0},{2,3},{3,2},{4,5},{5,4},{6,7},{7,6},{8,9},{9,8},{10,11... | collective-permute-start | bytes 3981320 | tf_op jit(solution)/shard_map/ppermute | solution.py:436
  75.4 2.2 %copy-done = bf16[2,1024,1024]{2,1,0:T(8,128)(2,1)S(1)} copy-done((bf16[2,1024,1024]{2,1,0:T(8,128)(2,1)S(1)}, bf16[2,1024,1024]{2,1,0:T(8,128)(2,1)}, u32[]{:S(2)}) %copy-start) | copy-done | bytes 4194328
  77.6 5.6 %second_mix.1 = bf16[256,8,512]{2,1,0:T(8,128)(2,1)} custom-call(bf16[64,32,512]{2,1,0:T(8,128)(2,1)S(1)} %all-to-all-done.r_hbm, bf16[2,1024,1024]{2,1,0:T(8,128)(2,1)S(1)} %copy-done), custom_call_target="tpu_custom_call" | custom-call | flops 2147483648 | bytes 8388608 | tf_op jit(solution)/shard_map/second_mix/pallas_call | solution.py:122
  83.3 0.9 copy-done.14
  84.1 12.7 %all-to-all-start.1 = ((bf16[256,8,512]{2,1,0:T(8,128)(2,1)}), bf16[256,8,512]{2,1,0:T(8,128)(2,1)}, u32[]{:S(2)}, u32[]{:S(2)}) async-start(bf16[256,8,512]{2,1,0:T(8,128)(2,1)} %second_mix.1), calls=%async_computation.1 | async-start | bytes 4194304 | tf_op jit(solution)/shard_map/all_to_all | solution.py:457
  97.1 1.0 slice.13
  98.1 1.5 collective-permute-start.15
  99.6 1.4 collective-permute-start.16
  101.0 1.0 dynamic-slice_bitcast_fusion
  102.0 3.7 %collective-permute-start.12 = (bf16[2,256,512]{2,1,0:T(8,128)(2,1)S(1)}, bf16[2,256,512]{2,1,0:T(8,128)(2,1)S(1)}, u32[]{:S(2)}, u32[]{:S(2)}) collective-permute-start(bf16[2,256,512]{2,1,0:T(8,128)(2,1)S(1)} %get-tuple-element.93), channel_id=1, source_target_pairs={{0,3},{1,2},{2,1},{3,0},{4,7},{5,6},{6,5},{7,4},{8,11},{9,10},{10,... | collective-permute-start | bytes 1572872 | tf_op jit(solution)/shard_map/ppermute | solution.py:435
  105.7 1.3 collective-permute-start.14
  107.1 6.5 %collective-permute-done.15.refs_11_ = bf16[320,512]{1,0:T(8,128)(2,1)} collective-permute-done((bf16[320,512]{1,0:T(8,128)(2,1)S(1)}, bf16[320,512]{1,0:T(8,128)(2,1)}, u32[]{:S(2)}, u32[]{:S(2)}) %collective-permute-start.15) | collective-permute-done | bytes 327712 | tf_op jit(solution)/shard_map/ppermute | solution.py:435
  113.7 3.7 %collective-permute-start.11 = (bf16[2,256,512]{2,1,0:T(8,128)(2,1)S(1)}, bf16[2,256,512]{2,1,0:T(8,128)(2,1)S(1)}, u32[]{:S(2)}, u32[]{:S(2)}) collective-permute-start(bf16[2,256,512]{2,1,0:T(8,128)(2,1)S(1)} %get-tuple-element.94), channel_id=1, source_target_pairs={{0,2},{1,3},{2,0},{3,1},{4,6},{5,7},{6,4},{7,5},{8,10},{9,11},{10,... | collective-permute-start | bytes 1572872 | tf_op jit(solution)/shard_map/ppermute | solution.py:435
  117.4 2.2 %collective-permute-start.10 = (bf16[2,256,512]{2,1,0:T(8,128)(2,1)S(1)}, bf16[2,256,512]{2,1,0:T(8,128)(2,1)S(1)}, u32[]{:S(2)}, u32[]{:S(2)}) collective-permute-start(bf16[2,256,512]{2,1,0:T(8,128)(2,1)S(1)} %get-tuple-element.95), channel_id=1, source_target_pairs={{0,1},{1,0},{2,3},{3,2},{4,5},{5,4},{6,7},{7,6},{8,9},{9,8},{10,11... | collective-permute-start | bytes 1572872 | tf_op jit(solution)/shard_map/ppermute | solution.py:435
  119.6 6.6 %collective-permute-done.12.x3 = bf16[2,256,512]{2,1,0:T(8,128)(2,1)S(1)} collective-permute-done((bf16[2,256,512]{2,1,0:T(8,128)(2,1)S(1)}, bf16[2,256,512]{2,1,0:T(8,128)(2,1)S(1)}, u32[]{:S(2)}, u32[]{:S(2)}) %collective-permute-start.12) | collective-permute-done | bytes 524320 | tf_op jit(solution)/shard_map/ppermute | solution.py:435
  126.2 3.6 %collective-permute-start.22 = (bf16[640,512]{1,0:T(8,128)(2,1)S(1)}, bf16[640,512]{1,0:T(8,128)(2,1)S(1)}, u32[]{:S(2)}, u32[]{:S(2)}) collective-permute-start(bf16[640,512]{1,0:T(8,128)(2,1)S(1)} %copy-done.12), channel_id=1, source_target_pairs={{0,1},{1,0},{2,3},{3,2},{4,5},{5,4},{6,7},{7,6},{8,9},{9,8},{10,11... | collective-permute-start | bytes 1966088 | tf_op jit(solution)/shard_map/ppermute | solution.py:436
  129.8 16.8 %collective-permute-done.11.x2 = bf16[2,256,512]{2,1,0:T(8,128)(2,1)S(1)} collective-permute-done((bf16[2,256,512]{2,1,0:T(8,128)(2,1)S(1)}, bf16[2,256,512]{2,1,0:T(8,128)(2,1)S(1)}, u32[]{:S(2)}, u32[]{:S(2)}) %collective-permute-start.11) | collective-permute-done | bytes 524320 | tf_op jit(solution)/shard_map/ppermute | solution.py:435
  148.5 0.9 collective-permute-done.20.refs_20_
  149.9 3.0 %collective-permute-done.23.refs_23_ = bf16[640,512]{1,0:T(8,128)(2,1)S(1)} collective-permute-done((bf16[640,512]{1,0:T(8,128)(2,1)S(1)}, bf16[640,512]{1,0:T(8,128)(2,1)S(1)}, u32[]{:S(2)}, u32[]{:S(2)}) %collective-permute-start.23) | collective-permute-done | bytes 655392 | tf_op jit(solution)/shard_map/ppermute | solution.py:436
  152.8 0.9 collective-permute-done.24.refs_24_
  155.7 18.9 %mlp.1 = bf16[2,256,2048]{2,1,0:T(8,128)(2,1)} custom-call(s32[2]{0:T(128)} %pad_add_fusion.meta, bf16[4,512,512]{2,1,0:T(8,128)(2,1)} %bitcast.5.r_hbm, bf16[2,256,512]{2,1,0:T(8,128)(2,1)} %get-tuple-element.77.x0, bf16[2,256,512]{2,1,0:T(8,128)(2,1)} %copy-done.22, bf16[2,256,512]{2,1,0:T(8,128)(2,1)} %copy-done.21, bf16[2,256,512]{2,1,0:T(8,128)(2,1)} %copy-done.20, ...), custom_call_target="tpu_custom_call" | custom-call | flops 11811160064 | bytes 27262976 | tf_op jit(solution)/shard_map/mlp/pallas_call | solution.py:368
  (79 shorter events, 7.3 us)
Async XLA Ops:
  4.6 67.1 %all-to-all-start = ((bf16[64,32,512]{2,1,0:T(8,128)(2,1)}), bf16[64,32,512]{2,1,0:T(8,128)(2,1)S(1)}, u32[]{:S(2)}, u32[]{:S(2)}) async-start(bf16[64,32,512]{2,1,0:T(8,128)(2,1)} %first_mix.1), calls=%async_computation | async-start | bytes 4194304 | tf_op jit(solution)/shard_map/all_to_all | solution.py:439
  24.5 17.1 %collective-permute-start = (bf16[656,512]{1,0:T(8,128)(2,1)}, bf16[656,512]{1,0:T(8,128)(2,1)S(1)}, u32[]{:S(2)}, u32[]{:S(2)}) collective-permute-start(bf16[656,512]{1,0:T(8,128)(2,1)} %get-tuple-element.50), channel_id=1, source_target_pairs={{0,6},{1,7},{2,4},{3,5},{4,2},{5,3},{6,0},{7,1},{8,14},{9,15},{10,... | collective-permute-start | bytes 2015240 | tf_op jit(solution)/shard_map/ppermute | solution.py:435
  26.8 28.9 %collective-permute-start.1 = (bf16[640,512]{1,0:T(8,128)(2,1)}, bf16[640,512]{1,0:T(8,128)(2,1)S(1)}, u32[]{:S(2)}, u32[]{:S(2)}) collective-permute-start(bf16[640,512]{1,0:T(8,128)(2,1)} %get-tuple-element.52), channel_id=1, source_target_pairs={{0,6},{1,7},{2,4},{3,5},{4,2},{5,3},{6,0},{7,1},{8,14},{9,15},{10,... | collective-permute-start | bytes 1966088 | tf_op jit(solution)/shard_map/ppermute | solution.py:435
  41.6 21.2 %copy-start.6 = (bf16[656,512]{1,0:T(8,128)(2,1)}, bf16[656,512]{1,0:T(8,128)(2,1)S(1)}, u32[]{:S(2)}) copy-start(bf16[656,512]{1,0:T(8,128)(2,1)S(1)} %collective-permute-done.refs_8_) | copy-start | bytes 2015236
  41.6 30.1 %collective-permute-start.4 = (bf16[656,512]{1,0:T(8,128)(2,1)S(1)}, bf16[656,512]{1,0:T(8,128)(2,1)S(1)}, u32[]{:S(2)}, u32[]{:S(2)}) collective-permute-start(bf16[656,512]{1,0:T(8,128)(2,1)S(1)} %collective-permute-done.refs_8_), channel_id=1, source_target_pairs={{0,192},{1,193},{2,194},{3,195},{4,196},{5,197},{6,198},{7,199},{8... | collective-permute-start | bytes 2015240 | tf_op jit(solution)/shard_map/ppermute | solution.py:435
  43.7 28.0 %collective-permute-start.3 = (bf16[656,512]{1,0:T(8,128)(2,1)S(1)}, bf16[656,512]{1,0:T(8,128)(2,1)}, u32[]{:S(2)}, u32[]{:S(2)}) collective-permute-start(bf16[656,512]{1,0:T(8,128)(2,1)S(1)} %collective-permute-done.refs_8_), channel_id=1, source_target_pairs={{0,64},{1,65},{2,66},{3,67},{4,68},{5,69},{6,70},{7,71},{8,72},{9,... | collective-permute-start | bytes 2015240 | tf_op jit(solution)/shard_map/ppermute | solution.py:435
  55.7 16.0 %collective-permute-start.2 = (bf16[640,512]{1,0:T(8,128)(2,1)}, bf16[640,512]{1,0:T(8,128)(2,1)S(1)}, u32[]{:S(2)}, u32[]{:S(2)}) collective-permute-start(bf16[640,512]{1,0:T(8,128)(2,1)} %get-tuple-element.54), channel_id=1, source_target_pairs={{0,6},{1,7},{2,4},{3,5},{4,2},{5,3},{6,0},{7,1},{8,14},{9,15},{10,... | collective-permute-start | bytes 1966088 | tf_op jit(solution)/shard_map/ppermute | solution.py:435
  71.7 76.5 %copy-start.2 = (bf16[656,512]{1,0:T(8,128)(2,1)}, bf16[656,512]{1,0:T(8,128)(2,1)S(1)}, u32[]{:S(2)}) copy-start(bf16[656,512]{1,0:T(8,128)(2,1)S(1)} %collective-permute-done.4.refs_10_) | copy-start | bytes 2015236
  71.8 12.4 %collective-permute-start.5 = (bf16[1296,512]{1,0:T(8,128)(2,1)}, bf16[1296,512]{1,0:T(8,128)(2,1)}, u32[]{:S(2)}, u32[]{:S(2)}) collective-permute-start(bf16[1296,512]{1,0:T(8,128)(2,1)} %get-tuple-element.61.refs_0_), channel_id=1, source_target_pairs={{0,1},{1,0},{2,3},{3,2},{4,5},{5,4},{6,7},{7,6},{8,9},{9,8},{10,11... | collective-permute-start | bytes 3981320 | tf_op jit(solution)/shard_map/ppermute | solution.py:436
  74.4 9.7 %collective-permute-start.6 = (bf16[1296,512]{1,0:T(8,128)(2,1)}, bf16[1296,512]{1,0:T(8,128)(2,1)}, u32[]{:S(2)}, u32[]{:S(2)}) collective-permute-start(bf16[1296,512]{1,0:T(8,128)(2,1)} %get-tuple-element.62.refs_1_), channel_id=1, source_target_pairs={{0,1},{1,0},{2,3},{3,2},{4,5},{5,4},{6,7},{7,6},{8,9},{9,8},{10,11... | collective-permute-start | bytes 3981320 | tf_op jit(solution)/shard_map/ppermute | solution.py:436
  74.5 9.6 %collective-permute-start.7 = (bf16[1296,512]{1,0:T(8,128)(2,1)}, bf16[1296,512]{1,0:T(8,128)(2,1)}, u32[]{:S(2)}, u32[]{:S(2)}) collective-permute-start(bf16[1296,512]{1,0:T(8,128)(2,1)} %get-tuple-element.63.refs_2_), channel_id=1, source_target_pairs={{0,1},{1,0},{2,3},{3,2},{4,5},{5,4},{6,7},{7,6},{8,9},{9,8},{10,11... | collective-permute-start | bytes 3981320 | tf_op jit(solution)/shard_map/ppermute | solution.py:436
  74.9 9.2 %collective-permute-start.8 = (bf16[1296,512]{1,0:T(8,128)(2,1)}, bf16[1296,512]{1,0:T(8,128)(2,1)}, u32[]{:S(2)}, u32[]{:S(2)}) collective-permute-start(bf16[1296,512]{1,0:T(8,128)(2,1)} %get-tuple-element.64.refs_3_), channel_id=1, source_target_pairs={{0,1},{1,0},{2,3},{3,2},{4,5},{5,4},{6,7},{7,6},{8,9},{9,8},{10,11... | collective-permute-start | bytes 3981320 | tf_op jit(solution)/shard_map/ppermute | solution.py:436
  75.0 8.2 %collective-permute-start.9 = (bf16[640,512]{1,0:T(8,128)(2,1)S(1)}, bf16[640,512]{1,0:T(8,128)(2,1)S(1)}, u32[]{:S(2)}, u32[]{:S(2)}) collective-permute-start(bf16[640,512]{1,0:T(8,128)(2,1)S(1)} %collective-permute-done.2.refs_16_), channel_id=1, source_target_pairs={{0,1},{1,0},{2,3},{3,2},{4,5},{5,4},{6,7},{7,6},{8,9},{9,8},{10,11... | collective-permute-start | bytes 1966088 | tf_op jit(solution)/shard_map/ppermute | solution.py:436
  83.2 17.7 %copy-start.1 = (bf16[2,1024,512]{2,1,0:T(8,128)(2,1)S(1)}, bf16[2,1024,512]{2,1,0:T(8,128)(2,1)}, u32[]{:S(2)}) copy-start(bf16[2,1024,512]{2,1,0:T(8,128)(2,1)} %param.9) | copy-start | bytes 6291460
  84.1 70.5 %all-to-all-start.1 = ((bf16[256,8,512]{2,1,0:T(8,128)(2,1)}), bf16[256,8,512]{2,1,0:T(8,128)(2,1)}, u32[]{:S(2)}, u32[]{:S(2)}) async-start(bf16[256,8,512]{2,1,0:T(8,128)(2,1)} %second_mix.1), calls=%async_computation.1 | async-start | bytes 4194304 | tf_op jit(solution)/shard_map/all_to_all | solution.py:457
  98.1 15.6 %collective-permute-start.15 = (bf16[320,512]{1,0:T(8,128)(2,1)S(1)}, bf16[320,512]{1,0:T(8,128)(2,1)}, u32[]{:S(2)}, u32[]{:S(2)}) collective-permute-start(bf16[320,512]{1,0:T(8,128)(2,1)S(1)} %slice.13), channel_id=1, source_target_pairs={{0,64},{1,65},{2,66},{3,67},{4,68},{5,69},{6,70},{7,71},{8,72},{9,... | collective-permute-start | bytes 983048 | tf_op jit(solution)/shard_map/ppermute | solution.py:435
  99.6 17.8 %collective-permute-start.16 = (bf16[336,512]{1,0:T(8,128)(2,1)S(1)}, bf16[336,512]{1,0:T(8,128)(2,1)}, u32[]{:S(2)}, u32[]{:S(2)}) collective-permute-start(bf16[336,512]{1,0:T(8,128)(2,1)S(1)} %slice.14), channel_id=1, source_target_pairs={{0,192},{1,193},{2,194},{3,195},{4,196},{5,197},{6,198},{7,199},{8... | collective-permute-start | bytes 1032200 | tf_op jit(solution)/shard_map/ppermute | solution.py:435
  101.0 46.6 %copy-start.7 = (bf16[656,512]{1,0:T(8,128)(2,1)S(1)}, bf16[656,512]{1,0:T(8,128)(2,1)}, u32[]{:S(2)}) copy-start(bf16[656,512]{1,0:T(8,128)(2,1)} %copy-done.6) | copy-start | bytes 2015236
  102.0 24.2 %collective-permute-start.12 = (bf16[2,256,512]{2,1,0:T(8,128)(2,1)S(1)}, bf16[2,256,512]{2,1,0:T(8,128)(2,1)S(1)}, u32[]{:S(2)}, u32[]{:S(2)}) collective-permute-start(bf16[2,256,512]{2,1,0:T(8,128)(2,1)S(1)} %get-tuple-element.93), channel_id=1, source_target_pairs={{0,3},{1,2},{2,1},{3,0},{4,7},{5,6},{6,5},{7,4},{8,11},{9,10},{10,... | collective-permute-start | bytes 1572872 | tf_op jit(solution)/shard_map/ppermute | solution.py:435
  105.7 40.9 %collective-permute-start.14 = (bf16[640,512]{1,0:T(8,128)(2,1)S(1)}, bf16[640,512]{1,0:T(8,128)(2,1)S(1)}, u32[]{:S(2)}, u32[]{:S(2)}) collective-permute-start(bf16[640,512]{1,0:T(8,128)(2,1)S(1)} %copy-done.12), channel_id=1, source_target_pairs={{0,192},{1,193},{2,194},{3,195},{4,196},{5,197},{6,198},{7,199},{8... | collective-permute-start | bytes 1966088 | tf_op jit(solution)/shard_map/ppermute | solution.py:435
  106.9 39.7 %collective-permute-start.13 = (bf16[640,512]{1,0:T(8,128)(2,1)S(1)}, bf16[640,512]{1,0:T(8,128)(2,1)S(1)}, u32[]{:S(2)}, u32[]{:S(2)}) collective-permute-start(bf16[640,512]{1,0:T(8,128)(2,1)S(1)} %copy-done.12), channel_id=1, source_target_pairs={{0,64},{1,65},{2,66},{3,67},{4,68},{5,69},{6,70},{7,71},{8,72},{9,... | collective-permute-start | bytes 1966088 | tf_op jit(solution)/shard_map/ppermute | solution.py:435
  113.7 32.9 %collective-permute-start.11 = (bf16[2,256,512]{2,1,0:T(8,128)(2,1)S(1)}, bf16[2,256,512]{2,1,0:T(8,128)(2,1)S(1)}, u32[]{:S(2)}, u32[]{:S(2)}) collective-permute-start(bf16[2,256,512]{2,1,0:T(8,128)(2,1)S(1)} %get-tuple-element.94), channel_id=1, source_target_pairs={{0,2},{1,3},{2,0},{3,1},{4,6},{5,7},{6,4},{7,5},{8,10},{9,11},{10,... | collective-permute-start | bytes 1572872 | tf_op jit(solution)/shard_map/ppermute | solution.py:435
  117.4 29.2 %collective-permute-start.10 = (bf16[2,256,512]{2,1,0:T(8,128)(2,1)S(1)}, bf16[2,256,512]{2,1,0:T(8,128)(2,1)S(1)}, u32[]{:S(2)}, u32[]{:S(2)}) collective-permute-start(bf16[2,256,512]{2,1,0:T(8,128)(2,1)S(1)} %get-tuple-element.95), channel_id=1, source_target_pairs={{0,1},{1,0},{2,3},{3,2},{4,5},{5,4},{6,7},{7,6},{8,9},{9,8},{10,11... | collective-permute-start | bytes 1572872 | tf_op jit(solution)/shard_map/ppermute | solution.py:435
  126.2 20.5 %copy-start.20 = (bf16[2,256,512]{2,1,0:T(8,128)(2,1)}, bf16[2,256,512]{2,1,0:T(8,128)(2,1)S(1)}, u32[]{:S(2)}) copy-start(bf16[2,256,512]{2,1,0:T(8,128)(2,1)S(1)} %collective-permute-done.12.x3) | copy-start | bytes 1572868
  126.2 22.0 %collective-permute-start.22 = (bf16[640,512]{1,0:T(8,128)(2,1)S(1)}, bf16[640,512]{1,0:T(8,128)(2,1)S(1)}, u32[]{:S(2)}, u32[]{:S(2)}) collective-permute-start(bf16[640,512]{1,0:T(8,128)(2,1)S(1)} %copy-done.12), channel_id=1, source_target_pairs={{0,1},{1,0},{2,3},{3,2},{4,5},{5,4},{6,7},{7,6},{8,9},{9,8},{10,11... | collective-permute-start | bytes 1966088 | tf_op jit(solution)/shard_map/ppermute | solution.py:436
  146.6 2.9 %collective-permute-start.21 = (bf16[336,512]{1,0:T(8,128)(2,1)}, bf16[336,512]{1,0:T(8,128)(2,1)}, u32[]{:S(2)}, u32[]{:S(2)}) collective-permute-start(bf16[336,512]{1,0:T(8,128)(2,1)} %collective-permute-done.16.refs_12_), channel_id=1, source_target_pairs={{0,1},{1,0},{2,3},{3,2},{4,5},{5,4},{6,7},{7,6},{8,9},{9,8},{10,11... | collective-permute-start | bytes 1032200 | tf_op jit(solution)/shard_map/ppermute | solution.py:436
  147.4 2.0 %collective-permute-start.20 = (bf16[320,512]{1,0:T(8,128)(2,1)}, bf16[320,512]{1,0:T(8,128)(2,1)}, u32[]{:S(2)}, u32[]{:S(2)}) collective-permute-start(bf16[320,512]{1,0:T(8,128)(2,1)} %collective-permute-done.15.refs_11_), channel_id=1, source_target_pairs={{0,1},{1,0},{2,3},{3,2},{4,5},{5,4},{6,7},{7,6},{8,9},{9,8},{10,11... | collective-permute-start | bytes 983048 | tf_op jit(solution)/shard_map/ppermute | solution.py:436
  147.6 6.2 %collective-permute-start.17 = (bf16[656,512]{1,0:T(8,128)(2,1)S(1)}, bf16[656,512]{1,0:T(8,128)(2,1)S(1)}, u32[]{:S(2)}, u32[]{:S(2)}) collective-permute-start(bf16[656,512]{1,0:T(8,128)(2,1)S(1)} %copy-done.7), channel_id=1, source_target_pairs={{0,1},{1,0},{2,3},{3,2},{4,5},{5,4},{6,7},{7,6},{8,9},{9,8},{10,11... | collective-permute-start | bytes 2015240 | tf_op jit(solution)/shard_map/ppermute | solution.py:436
  147.9 5.9 %collective-permute-start.18 = (bf16[656,512]{1,0:T(8,128)(2,1)}, bf16[656,512]{1,0:T(8,128)(2,1)S(1)}, u32[]{:S(2)}, u32[]{:S(2)}) collective-permute-start(bf16[656,512]{1,0:T(8,128)(2,1)} %collective-permute-done.3.refs_9_), channel_id=1, source_target_pairs={{0,1},{1,0},{2,3},{3,2},{4,5},{5,4},{6,7},{7,6},{8,9},{9,8},{10,11... | collective-permute-start | bytes 2015240 | tf_op jit(solution)/shard_map/ppermute | solution.py:436
  148.2 6.4 %collective-permute-start.19 = (bf16[656,512]{1,0:T(8,128)(2,1)S(1)}, bf16[656,512]{1,0:T(8,128)(2,1)S(1)}, u32[]{:S(2)}, u32[]{:S(2)}) collective-permute-start(bf16[656,512]{1,0:T(8,128)(2,1)S(1)} %collective-permute-done.4.refs_10_), channel_id=1, source_target_pairs={{0,1},{1,0},{2,3},{3,2},{4,5},{5,4},{6,7},{7,6},{8,9},{9,8},{10,11... | collective-permute-start | bytes 2015240 | tf_op jit(solution)/shard_map/ppermute | solution.py:436
  149.4 3.5 %collective-permute-start.23 = (bf16[640,512]{1,0:T(8,128)(2,1)S(1)}, bf16[640,512]{1,0:T(8,128)(2,1)S(1)}, u32[]{:S(2)}, u32[]{:S(2)}) collective-permute-start(bf16[640,512]{1,0:T(8,128)(2,1)S(1)} %collective-permute-done.13.refs_14_), channel_id=1, source_target_pairs={{0,1},{1,0},{2,3},{3,2},{4,5},{5,4},{6,7},{7,6},{8,9},{9,8},{10,11... | collective-permute-start | bytes 1966088 | tf_op jit(solution)/shard_map/ppermute | solution.py:436
  149.5 4.3 %collective-permute-start.24 = (bf16[640,512]{1,0:T(8,128)(2,1)S(1)}, bf16[640,512]{1,0:T(8,128)(2,1)S(1)}, u32[]{:S(2)}, u32[]{:S(2)}) collective-permute-start(bf16[640,512]{1,0:T(8,128)(2,1)S(1)} %collective-permute-done.14.refs_15_), channel_id=1, source_target_pairs={{0,1},{1,0},{2,3},{3,2},{4,5},{5,4},{6,7},{7,6},{8,9},{9,8},{10,11... | collective-permute-start | bytes 1966088 | tf_op jit(solution)/shard_map/ppermute | solution.py:436
  (18 other events, 95.9 us)
where the time goes:
time: 175 us
  waiting for transfers between devices  62.4 us (36%)
  starting transfers between devices  56 us (32%)
  Pallas kernels  46.7 us (27%)
  local copies, waits for them, and re-layouts  7.82 us (4%)
    ppermute x12, waiting for transfers between devices, on_device(): move = lambda piece, to: lax.ppermute(piece, BOTH, to)  57.6 us
    ppermute x12, starting transfers between devices, on_device(): move = lambda piece, to: lax.ppermute(piece, BOTH, to)  20.8 us
    pallas_call x1, Pallas kernels, mlp(): pl.pallas_call(mlp_kernel, out_shape=jax.ShapeDtypeStruct((2, 256, 2048),...  18.9 us
    all_to_all x1, starting transfers between devices, on_device(): lax.all_to_all(sent, 'seq', split_axis=0, concat_axis=0, tiled=True)  13.6 us
    all_to_all x1, starting transfers between devices, on_device(): lax.all_to_all(turned, ('chan', 'seq'), split_axis=0, concat_axis=0, tile...  12.7 us
    ppermute x13, starting transfers between devices, on_device(): swap = lambda piece: lax.ppermute(piece, BOTH, TO_CORE)  8.84 us
    pallas_call x1, Pallas kernels, pack(): pl.pallas_call(pack_kernel, out_shape=(jax.ShapeDtypeStruct((A_ROWS + B_R...  7.61 us
    unnamed x46, local copies, waits for them, and re-layouts  5.83 us
  transfers between devices with their start and end apart: 27, of which 9 were waited for; matrix products, arithmetic and copies ran while one was open for 2% of the time, Pallas kernels for 13%

commit v1 on v0

--- a/solution.py
+++ b/solution.py
@@ -158,16 +158,12 @@
     return jnp.concatenate(rows + [jnp.zeros((10, 512), F32)], axis=0).astype(BF16)
 
 
-def quarter_kernel(meta, g_ref, w1, w2, w3, w4, a_ref, b_ref, f_ref, v1, v2, v3, v5, v4, sem):
+def quarter_a_kernel(meta, g_ref, w1, w2, a_ref, v1, v2, sem):
     y = meta[1]
-    far = (y + 2) % 4
-    near_at, far_at = pl.multiple_of(y * 512, 512), pl.multiple_of(far * 512, 512)
+    at = pl.multiple_of(y * 512, 512)
     copies = [
         pltpu.make_async_copy(w1.at[0], v1, sem.at[0]),
-        pltpu.make_async_copy(w2.at[0, pl.ds(near_at, 512), :], v2, sem.at[1]),
-        pltpu.make_async_copy(w3.at[0, :, pl.ds(near_at, 512)], v3, sem.at[2]),
-        pltpu.make_async_copy(w3.at[0, :, pl.ds(far_at, 512)], v5, sem.at[3]),
-        pltpu.make_async_copy(w4.at[0], v4, sem.at[4]),
+        pltpu.make_async_copy(w2.at[0, pl.ds(at, 512), :], v2, sem.at[1]),
     ]
     for c in copies:
         c.start()
@@ -176,23 +172,51 @@
     a_ref[0:128, :] = mm_nt(same_rows(128, y * 128), v1[...]).astype(BF16)
     a_ref[128:640, :] = mm_nt(turned_rows(512, 0), v2[...]).astype(BF16)
     a_ref[640:656, :] = gate_rows(g_ref)
+
+
+def quarter_a(meta, gate, w1, w2):
+    return pl.pallas_call(
+        quarter_a_kernel,
+        out_shape=jax.ShapeDtypeStruct((A_ROWS, 512), BF16),
+        in_specs=[SMEM, VMEM, HBM, HBM],
+        out_specs=VMEM,
+        scratch_shapes=[pltpu.VMEM((512, 512), BF16)] * 2 + [pltpu.SemaphoreType.DMA((2,))],
+        compiler_params=params(FULL),
+        cost_estimate=pl.CostEstimate(flops=2**28, bytes_accessed=2 * MIB, transcendentals=0),
+        name="quarter_a",
+    )(meta, gate, w1, w2)
+
+
+def quarter_b_kernel(meta, w3, w4, b_ref, f_ref, v3, v5, v4, sem):
+    y = meta[1]
+    far = (y + 2) % 4
+    near_at, far_at = pl.multiple_of(y * 512, 512), pl.multiple_of(far * 512, 512)
+    copies = [
+        pltpu.make_async_copy(w3.at[0, :, pl.ds(near_at, 512)], v3, sem.at[0]),
+        pltpu.make_async_copy(w3.at[0, :, pl.ds(far_at, 512)], v5, sem.at[1]),
+        pltpu.make_async_copy(w4.at[0], v4, sem.at[2]),
+    ]
+    for c in copies:
+        c.start()
+    for c in copies:
+        c.wait()
     for at, v, out in ((y, v3, b_ref), (far, v5, f_ref)):
         out[0:512, :] = mm_nt(same_rows(512, 0), v[...]).astype(BF16)
         out[512:640, :] = mm_nt(turned_rows(128, at * 128), v4[...]).astype(BF16)
 
 
-def quarter(meta, gate, w1, w2, w3, w4):
-    b_piece = jax.ShapeDtypeStruct((B_ROWS, 512), BF16)
-    return pl.pallas_call(
-        quarter_kernel,
-        out_shape=(jax.ShapeDtypeStruct((A_ROWS, 512), BF16), b_piece, b_piece),
-        in_specs=[SMEM, VMEM] + [HBM] * 4,
-        out_specs=(VMEM, VMEM, VMEM),
-        scratch_shapes=[pltpu.VMEM((512, 512), BF16)] * 5 + [pltpu.SemaphoreType.DMA((5,))],
+def quarter_b(meta, w3, w4):
+    piece = jax.ShapeDtypeStruct((B_ROWS, 512), BF16)
+    return pl.pallas_call(
+        quarter_b_kernel,
+        out_shape=(piece, piece),
+        in_specs=[SMEM, HBM, HBM],
+        out_specs=(VMEM, VMEM),
+        scratch_shapes=[pltpu.VMEM((512, 512), BF16)] * 3 + [pltpu.SemaphoreType.DMA((3,))],
         compiler_params=params(FULL),
-        cost_estimate=pl.CostEstimate(flops=2**29, bytes_accessed=4 * MIB, transcendentals=0),
-        name="quarter",
-    )(meta, gate, w1, w2, w3, w4)
+        cost_estimate=pl.CostEstimate(flops=2**28, bytes_accessed=3 * MIB, transcendentals=0),
+        name="quarter_b",
+    )(meta, w3, w4)
 
 
 def pack_kernel(meta, g_ref, w1, w2, w3, w4, *o_refs):
@@ -438,8 +462,9 @@
     sent = first_mix(grouped, mix_first)
     received = lax.all_to_all(sent, "seq", split_axis=0, concat_axis=0, tiled=True)
     _, meta = bar((sent, meta))
-    mine_a, mine_b, mine_far = quarter(meta, gate, up_first, up_second, down_first, down_second)
+    mine_a = quarter_a(meta, gate, up_first, up_second)
     _, meta = bar((mine_a, meta))
+    mine_b, mine_far = quarter_b(meta, down_first, down_second)
     near_a, near_b = move(mine_a, TO_X), move(mine_b, TO_X)
     _, mine_far = bar((near_b, mine_far))
     far_b = move(mine_far, TO_X)

time: 175 us -> 174 us (level)
  waiting for transfers between devices: 62.4 us -> 58.3 us
  Pallas kernels: 46.7 us -> 49.1 us
    ppermute x12, waiting for transfers between devices: 57.6 us -> 53.5 us  [on_device(): move = lambda piece, to: lax.ppermute(piece, BOTH, to)]
    pallas_call x1 -> x2, Pallas kernels: 4.97 us -> 7.44 us  [the longest x1 4.01 us: quarter_b(): pl.pallas_call(quarter_b_kernel, out_shape=(piece, piece), in_specs=[SMEM...]
  transfers between devices with their start and end apart: 27 -> 27, of which waited for: 9 -> 9; matrix products, arithmetic and copies ran while one was open for 2% -> 2% of each run, Pallas kernels for 13% -> 15%
where the time goes in v1:
time: 174 us; the launch traced here: 173 us
  waiting for transfers between devices  58.3 us (34%)
  starting transfers between devices  56.1 us (32%)
  Pallas kernels  49.1 us (28%)
  local copies, waits for them, and re-layouts  7.81 us (4%)
    ppermute x12, waiting for transfers between devices, on_device(): move = lambda piece, to: lax.ppermute(piece, BOTH, to)  53.5 us
    ppermute x12, starting transfers between devices, on_device(): move = lambda piece, to: lax.ppermute(piece, BOTH, to)  20.9 us
    pallas_call x1, Pallas kernels, mlp(): pl.pallas_call(mlp_kernel, out_shape=jax.ShapeDtypeStruct((2, 256, 2048),...  18.9 us
    all_to_all x1, starting transfers between devices, on_device(): lax.all_to_all(sent, 'seq', split_axis=0, concat_axis=0, tiled=True)  13.6 us
    all_to_all x1, starting transfers between devices, on_device(): lax.all_to_all(turned, ('chan', 'seq'), split_axis=0, concat_axis=0, tile...  12.7 us
    ppermute x13, starting transfers between devices, on_device(): swap = lambda piece: lax.ppermute(piece, BOTH, TO_CORE)  8.84 us
    pallas_call x1, Pallas kernels, pack(): pl.pallas_call(pack_kernel, out_shape=(jax.ShapeDtypeStruct((A_ROWS + B_R...  7.62 us
    unnamed x46, local copies, waits for them, and re-layouts  5.83 us
  transfers between devices with their start and end apart: 27, of which 9 were waited for; matrix products, arithmetic and copies ran while one was open for 2% of the time, Pallas kernels for 15%

profile of v1, /device:TPU:1, one launch (start us, length us, event | category | flops | bytes accessed | tf_op | source)
XLA Modules:
  0.0 173.3 jit_solution(8103422514109105890)
XLA Ops:
  0.0 4.6 %first_mix.1 = bf16[64,32,512]{2,1,0:T(8,128)(2,1)} custom-call(bf16[2,4,256,512]{3,2,1,0:T(8,128)(2,1)} %bitcast.16, bf16[4,256,256]{2,1,0:T(8,128)(2,1)} %m_hbm.1), custom_call_target="tpu_custom_call" | custom-call | flops 536870912 | bytes 5242880 | tf_op jit(solution)/shard_map/first_mix/pallas_call | solution.py:61
  4.6 13.6 %all-to-all-start = ((bf16[64,32,512]{2,1,0:T(8,128)(2,1)}), bf16[64,32,512]{2,1,0:T(8,128)(2,1)S(1)}, u32[]{:S(2)}, u32[]{:S(2)}) async-start(bf16[64,32,512]{2,1,0:T(8,128)(2,1)} %first_mix.1), calls=%async_computation | async-start | bytes 4194304 | tf_op jit(solution)/shard_map/all_to_all | solution.py:463
  19.5 3.4 %quarter_a.1 = bf16[656,512]{1,0:T(8,128)(2,1)} custom-call(s32[2]{0:T(128)} %pad_add_fusion.meta, f32[2,512]{1,0:T(2,128)} %pad_maximum_fusion.g_ref, bf16[1,512,512]{2,1,0:T(8,128)(2,1)} %w1.3, bf16[1,2048,512]{2,1,0:T(8,128)(2,1)} %w2.3), custom_call_target="tpu_custom_call" | custom-call | flops 268435456 | bytes 2097152 | tf_op jit(solution)/shard_map/quarter_a/pallas_call | solution.py:178
  22.9 2.4 %collective-permute-start = (bf16[656,512]{1,0:T(8,128)(2,1)}, bf16[656,512]{1,0:T(8,128)(2,1)S(1)}, u32[]{:S(2)}, u32[]{:S(2)}) collective-permute-start(bf16[656,512]{1,0:T(8,128)(2,1)} %quarter_a.1), channel_id=1, source_target_pairs={{0,6},{1,7},{2,4},{3,5},{4,2},{5,3},{6,0},{7,1},{8,14},{9,15},{10,... | collective-permute-start | bytes 2015240 | tf_op jit(solution)/shard_map/ppermute | solution.py:459
  25.3 4.0 %quarter_b.1 = (bf16[640,512]{1,0:T(8,128)(2,1)}, bf16[640,512]{1,0:T(8,128)(2,1)}) custom-call(s32[2]{0:T(128)} %pad_add_fusion.meta, bf16[1,512,2048]{2,1,0:T(8,128)(2,1)} %w3.3, bf16[1,512,512]{2,1,0:T(8,128)(2,1)} %w4.3), custom_call_target="tpu_custom_call" | custom-call | flops 268435456 | bytes 3145728 | tf_op jit(solution)/shard_map/quarter_b/pallas_call | solution.py:210
  29.8 10.3 %collective-permute-done.refs_8_ = bf16[656,512]{1,0:T(8,128)(2,1)S(1)} collective-permute-done((bf16[656,512]{1,0:T(8,128)(2,1)}, bf16[656,512]{1,0:T(8,128)(2,1)S(1)}, u32[]{:S(2)}, u32[]{:S(2)}) %collective-permute-start) | collective-permute-done | bytes 671776 | tf_op jit(solution)/shard_map/ppermute | solution.py:459
  40.1 2.1 %collective-permute-start.4 = (bf16[656,512]{1,0:T(8,128)(2,1)S(1)}, bf16[656,512]{1,0:T(8,128)(2,1)S(1)}, u32[]{:S(2)}, u32[]{:S(2)}) collective-permute-start(bf16[656,512]{1,0:T(8,128)(2,1)S(1)} %collective-permute-done.refs_8_), channel_id=1, source_target_pairs={{0,192},{1,193},{2,194},{3,195},{4,196},{5,197},{6,198},{7,199},{8... | collective-permute-start | bytes 2015240 | tf_op jit(solution)/shard_map/ppermute | solution.py:459
  42.2 12.0 %collective-permute-done.1.refs_13_ = bf16[640,512]{1,0:T(8,128)(2,1)S(1)} collective-permute-done((bf16[640,512]{1,0:T(8,128)(2,1)}, bf16[640,512]{1,0:T(8,128)(2,1)S(1)}, u32[]{:S(2)}, u32[]{:S(2)}) %collective-permute-start.1) | collective-permute-done | bytes 655392 | tf_op jit(solution)/shard_map/ppermute | solution.py:459
  54.2 2.0 %collective-permute-start.2 = (bf16[640,512]{1,0:T(8,128)(2,1)}, bf16[640,512]{1,0:T(8,128)(2,1)S(1)}, u32[]{:S(2)}, u32[]{:S(2)}) collective-permute-start(bf16[640,512]{1,0:T(8,128)(2,1)} %get-tuple-element.52), channel_id=1, source_target_pairs={{0,6},{1,7},{2,4},{3,5},{4,2},{5,3},{6,0},{7,1},{8,14},{9,15},{10,... | collective-permute-start | bytes 1966088 | tf_op jit(solution)/shard_map/ppermute | solution.py:459
  56.2 5.0 %spread.1.m_hbm = bf16[2,1024,1024]{2,1,0:T(8,128)(2,1)} custom-call(s32[2]{0:T(128)} %pad_add_fusion.meta, bf16[4,256,256]{2,1,0:T(8,128)(2,1)} %m_ref.1), custom_call_target="tpu_custom_call" | custom-call | flops 1073741824 | bytes 5242880 | tf_op jit(solution)/shard_map/spread/pallas_call | solution.py:92
  61.2 7.6 %pack.1 = (bf16[1296,512]{1,0:T(8,128)(2,1)}, bf16[1296,512]{1,0:T(8,128)(2,1)}, bf16[1296,512]{1,0:T(8,128)(2,1)}, bf16[1296,512]{1,0:T(8,128)(2,1)}) custom-call(s32[2]{0:T(128)} %pad_add_fusion.meta, f32[2,512]{1,0:T(2,128)} %pad_maximum_fusion.g_ref, bf16[1,512,512]{2,1,0:T(8,128)(2,1)} %w1.3, bf16[1,2048,512]{2,1,0:T(8,128)(2,1)} %w2.3, ...), custom_call_target="tpu_custom_call" | custom-call | flops 2147483648 | bytes 10485760 | tf_op jit(solution)/shard_map/pack/pallas_call | solution.py:237
  68.8 1.4 collective-permute-done.2.refs_16_
  70.2 2.7 %collective-permute-start.5 = (bf16[1296,512]{1,0:T(8,128)(2,1)}, bf16[1296,512]{1,0:T(8,128)(2,1)}, u32[]{:S(2)}, u32[]{:S(2)}) collective-permute-start(bf16[1296,512]{1,0:T(8,128)(2,1)} %get-tuple-element.59.refs_0_), channel_id=1, source_target_pairs={{0,1},{1,0},{2,3},{3,2},{4,5},{5,4},{6,7},{7,6},{8,9},{9,8},{10,11... | collective-permute-start | bytes 3981320 | tf_op jit(solution)/shard_map/ppermute | solution.py:460
  73.9 2.2 %copy-done = bf16[2,1024,1024]{2,1,0:T(8,128)(2,1)S(1)} copy-done((bf16[2,1024,1024]{2,1,0:T(8,128)(2,1)S(1)}, bf16[2,1024,1024]{2,1,0:T(8,128)(2,1)}, u32[]{:S(2)}) %copy-start) | copy-done | bytes 4194328
  76.1 5.5 %second_mix.1 = bf16[256,8,512]{2,1,0:T(8,128)(2,1)} custom-call(bf16[64,32,512]{2,1,0:T(8,128)(2,1)S(1)} %all-to-all-done.r_hbm, bf16[2,1024,1024]{2,1,0:T(8,128)(2,1)S(1)} %copy-done), custom_call_target="tpu_custom_call" | custom-call | flops 2147483648 | bytes 8388608 | tf_op jit(solution)/shard_map/second_mix/pallas_call | solution.py:122
  81.7 0.9 copy-done.14
  82.6 12.7 %all-to-all-start.1 = ((bf16[256,8,512]{2,1,0:T(8,128)(2,1)}), bf16[256,8,512]{2,1,0:T(8,128)(2,1)}, u32[]{:S(2)}, u32[]{:S(2)}) async-start(bf16[256,8,512]{2,1,0:T(8,128)(2,1)} %second_mix.1), calls=%async_computation.1 | async-start | bytes 4194304 | tf_op jit(solution)/shard_map/all_to_all | solution.py:482
  95.5 1.0 slice.13
  96.5 1.5 collective-permute-start.15
  98.0 1.4 collective-permute-start.16
  99.4 1.0 dynamic-slice_bitcast_fusion
  100.4 3.7 %collective-permute-start.12 = (bf16[2,256,512]{2,1,0:T(8,128)(2,1)S(1)}, bf16[2,256,512]{2,1,0:T(8,128)(2,1)S(1)}, u32[]{:S(2)}, u32[]{:S(2)}) collective-permute-start(bf16[2,256,512]{2,1,0:T(8,128)(2,1)S(1)} %get-tuple-element.91), channel_id=1, source_target_pairs={{0,3},{1,2},{2,1},{3,0},{4,7},{5,6},{6,5},{7,4},{8,11},{9,10},{10,... | collective-permute-start | bytes 1572872 | tf_op jit(solution)/shard_map/ppermute | solution.py:459
  104.1 1.3 collective-permute-start.14
  105.6 6.5 %collective-permute-done.15.refs_11_ = bf16[320,512]{1,0:T(8,128)(2,1)} collective-permute-done((bf16[320,512]{1,0:T(8,128)(2,1)S(1)}, bf16[320,512]{1,0:T(8,128)(2,1)}, u32[]{:S(2)}, u32[]{:S(2)}) %collective-permute-start.15) | collective-permute-done | bytes 327712 | tf_op jit(solution)/shard_map/ppermute | solution.py:459
  112.1 3.7 %collective-permute-start.11 = (bf16[2,256,512]{2,1,0:T(8,128)(2,1)S(1)}, bf16[2,256,512]{2,1,0:T(8,128)(2,1)S(1)}, u32[]{:S(2)}, u32[]{:S(2)}) collective-permute-start(bf16[2,256,512]{2,1,0:T(8,128)(2,1)S(1)} %get-tuple-element.92), channel_id=1, source_target_pairs={{0,2},{1,3},{2,0},{3,1},{4,6},{5,7},{6,4},{7,5},{8,10},{9,11},{10,... | collective-permute-start | bytes 1572872 | tf_op jit(solution)/shard_map/ppermute | solution.py:459
  115.8 2.2 %collective-permute-start.10 = (bf16[2,256,512]{2,1,0:T(8,128)(2,1)S(1)}, bf16[2,256,512]{2,1,0:T(8,128)(2,1)S(1)}, u32[]{:S(2)}, u32[]{:S(2)}) collective-permute-start(bf16[2,256,512]{2,1,0:T(8,128)(2,1)S(1)} %get-tuple-element.93), channel_id=1, source_target_pairs={{0,1},{1,0},{2,3},{3,2},{4,5},{5,4},{6,7},{7,6},{8,9},{9,8},{10,11... | collective-permute-start | bytes 1572872 | tf_op jit(solution)/shard_map/ppermute | solution.py:459
  118.1 6.6 %collective-permute-done.12.x3 = bf16[2,256,512]{2,1,0:T(8,128)(2,1)S(1)} collective-permute-done((bf16[2,256,512]{2,1,0:T(8,128)(2,1)S(1)}, bf16[2,256,512]{2,1,0:T(8,128)(2,1)S(1)}, u32[]{:S(2)}, u32[]{:S(2)}) %collective-permute-start.12) | collective-permute-done | bytes 524320 | tf_op jit(solution)/shard_map/ppermute | solution.py:459
  124.6 3.6 %collective-permute-start.22 = (bf16[640,512]{1,0:T(8,128)(2,1)S(1)}, bf16[640,512]{1,0:T(8,128)(2,1)S(1)}, u32[]{:S(2)}, u32[]{:S(2)}) collective-permute-start(bf16[640,512]{1,0:T(8,128)(2,1)S(1)} %copy-done.12), channel_id=1, source_target_pairs={{0,1},{1,0},{2,3},{3,2},{4,5},{5,4},{6,7},{7,6},{8,9},{9,8},{10,11... | collective-permute-start | bytes 1966088 | tf_op jit(solution)/shard_map/ppermute | solution.py:460
  128.3 16.8 %collective-permute-done.11.x2 = bf16[2,256,512]{2,1,0:T(8,128)(2,1)S(1)} collective-permute-done((bf16[2,256,512]{2,1,0:T(8,128)(2,1)S(1)}, bf16[2,256,512]{2,1,0:T(8,128)(2,1)S(1)}, u32[]{:S(2)}, u32[]{:S(2)}) %collective-permute-start.11) | collective-permute-done | bytes 524320 | tf_op jit(solution)/shard_map/ppermute | solution.py:459
  148.3 3.0 %collective-permute-done.23.refs_23_ = bf16[640,512]{1,0:T(8,128)(2,1)S(1)} collective-permute-done((bf16[640,512]{1,0:T(8,128)(2,1)S(1)}, bf16[640,512]{1,0:T(8,128)(2,1)S(1)}, u32[]{:S(2)}, u32[]{:S(2)}) %collective-permute-start.23) | collective-permute-done | bytes 655392 | tf_op jit(solution)/shard_map/ppermute | solution.py:460
  151.3 0.9 collective-permute-done.24.refs_24_
  154.2 18.9 %mlp.1 = bf16[2,256,2048]{2,1,0:T(8,128)(2,1)} custom-call(s32[2]{0:T(128)} %pad_add_fusion.meta, bf16[4,512,512]{2,1,0:T(8,128)(2,1)} %bitcast.5.r_hbm, bf16[2,256,512]{2,1,0:T(8,128)(2,1)} %get-tuple-element.75.x0, bf16[2,256,512]{2,1,0:T(8,128)(2,1)} %copy-done.22, bf16[2,256,512]{2,1,0:T(8,128)(2,1)} %copy-done.21, bf16[2,256,512]{2,1,0:T(8,128)(2,1)} %copy-done.20, ...), custom_call_target="tpu_custom_call" | custom-call | flops 11811160064 | bytes 27262976 | tf_op jit(solution)/shard_map/mlp/pallas_call | solution.py:392
  (80 shorter events, 8.2 us)
Async XLA Ops:
  4.6 65.6 %all-to-all-start = ((bf16[64,32,512]{2,1,0:T(8,128)(2,1)}), bf16[64,32,512]{2,1,0:T(8,128)(2,1)S(1)}, u32[]{:S(2)}, u32[]{:S(2)}) async-start(bf16[64,32,512]{2,1,0:T(8,128)(2,1)} %first_mix.1), calls=%async_computation | async-start | bytes 4194304 | tf_op jit(solution)/shard_map/all_to_all | solution.py:463
  22.9 17.1 %collective-permute-start = (bf16[656,512]{1,0:T(8,128)(2,1)}, bf16[656,512]{1,0:T(8,128)(2,1)S(1)}, u32[]{:S(2)}, u32[]{:S(2)}) collective-permute-start(bf16[656,512]{1,0:T(8,128)(2,1)} %quarter_a.1), channel_id=1, source_target_pairs={{0,6},{1,7},{2,4},{3,5},{4,2},{5,3},{6,0},{7,1},{8,14},{9,15},{10,... | collective-permute-start | bytes 2015240 | tf_op jit(solution)/shard_map/ppermute | solution.py:459
  29.3 24.9 %collective-permute-start.1 = (bf16[640,512]{1,0:T(8,128)(2,1)}, bf16[640,512]{1,0:T(8,128)(2,1)S(1)}, u32[]{:S(2)}, u32[]{:S(2)}) collective-permute-start(bf16[640,512]{1,0:T(8,128)(2,1)} %get-tuple-element.50), channel_id=1, source_target_pairs={{0,6},{1,7},{2,4},{3,5},{4,2},{5,3},{6,0},{7,1},{8,14},{9,15},{10,... | collective-permute-start | bytes 1966088 | tf_op jit(solution)/shard_map/ppermute | solution.py:459
  40.1 21.2 %copy-start.6 = (bf16[656,512]{1,0:T(8,128)(2,1)}, bf16[656,512]{1,0:T(8,128)(2,1)S(1)}, u32[]{:S(2)}) copy-start(bf16[656,512]{1,0:T(8,128)(2,1)S(1)} %collective-permute-done.refs_8_) | copy-start | bytes 2015236
  40.1 30.1 %collective-permute-start.4 = (bf16[656,512]{1,0:T(8,128)(2,1)S(1)}, bf16[656,512]{1,0:T(8,128)(2,1)S(1)}, u32[]{:S(2)}, u32[]{:S(2)}) collective-permute-start(bf16[656,512]{1,0:T(8,128)(2,1)S(1)} %collective-permute-done.refs_8_), channel_id=1, source_target_pairs={{0,192},{1,193},{2,194},{3,195},{4,196},{5,197},{6,198},{7,199},{8... | collective-permute-start | bytes 2015240 | tf_op jit(solution)/shard_map/ppermute | solution.py:459
  42.2 28.0 %collective-permute-start.3 = (bf16[656,512]{1,0:T(8,128)(2,1)S(1)}, bf16[656,512]{1,0:T(8,128)(2,1)}, u32[]{:S(2)}, u32[]{:S(2)}) collective-permute-start(bf16[656,512]{1,0:T(8,128)(2,1)S(1)} %collective-permute-done.refs_8_), channel_id=1, source_target_pairs={{0,64},{1,65},{2,66},{3,67},{4,68},{5,69},{6,70},{7,71},{8,72},{9,... | collective-permute-start | bytes 2015240 | tf_op jit(solution)/shard_map/ppermute | solution.py:459
  54.2 16.0 %collective-permute-start.2 = (bf16[640,512]{1,0:T(8,128)(2,1)}, bf16[640,512]{1,0:T(8,128)(2,1)S(1)}, u32[]{:S(2)}, u32[]{:S(2)}) collective-permute-start(bf16[640,512]{1,0:T(8,128)(2,1)} %get-tuple-element.52), channel_id=1, source_target_pairs={{0,6},{1,7},{2,4},{3,5},{4,2},{5,3},{6,0},{7,1},{8,14},{9,15},{10,... | collective-permute-start | bytes 1966088 | tf_op jit(solution)/shard_map/ppermute | solution.py:459
  70.2 76.5 %copy-start.2 = (bf16[656,512]{1,0:T(8,128)(2,1)}, bf16[656,512]{1,0:T(8,128)(2,1)S(1)}, u32[]{:S(2)}) copy-start(bf16[656,512]{1,0:T(8,128)(2,1)S(1)} %collective-permute-done.4.refs_10_) | copy-start | bytes 2015236
  70.2 12.4 %collective-permute-start.5 = (bf16[1296,512]{1,0:T(8,128)(2,1)}, bf16[1296,512]{1,0:T(8,128)(2,1)}, u32[]{:S(2)}, u32[]{:S(2)}) collective-permute-start(bf16[1296,512]{1,0:T(8,128)(2,1)} %get-tuple-element.59.refs_0_), channel_id=1, source_target_pairs={{0,1},{1,0},{2,3},{3,2},{4,5},{5,4},{6,7},{7,6},{8,9},{9,8},{10,11... | collective-permute-start | bytes 3981320 | tf_op jit(solution)/shard_map/ppermute | solution.py:460
  72.9 9.7 %collective-permute-start.6 = (bf16[1296,512]{1,0:T(8,128)(2,1)}, bf16[1296,512]{1,0:T(8,128)(2,1)}, u32[]{:S(2)}, u32[]{:S(2)}) collective-permute-start(bf16[1296,512]{1,0:T(8,128)(2,1)} %get-tuple-element.60.refs_1_), channel_id=1, source_target_pairs={{0,1},{1,0},{2,3},{3,2},{4,5},{5,4},{6,7},{7,6},{8,9},{9,8},{10,11... | collective-permute-start | bytes 3981320 | tf_op jit(solution)/shard_map/ppermute | solution.py:460
  73.2 9.4 %collective-permute-start.7 = (bf16[1296,512]{1,0:T(8,128)(2,1)}, bf16[1296,512]{1,0:T(8,128)(2,1)}, u32[]{:S(2)}, u32[]{:S(2)}) collective-permute-start(bf16[1296,512]{1,0:T(8,128)(2,1)} %get-tuple-element.61.refs_2_), channel_id=1, source_target_pairs={{0,1},{1,0},{2,3},{3,2},{4,5},{5,4},{6,7},{7,6},{8,9},{9,8},{10,11... | collective-permute-start | bytes 3981320 | tf_op jit(solution)/shard_map/ppermute | solution.py:460
  73.4 9.2 %collective-permute-start.8 = (bf16[1296,512]{1,0:T(8,128)(2,1)}, bf16[1296,512]{1,0:T(8,128)(2,1)}, u32[]{:S(2)}, u32[]{:S(2)}) collective-permute-start(bf16[1296,512]{1,0:T(8,128)(2,1)} %get-tuple-element.62.refs_3_), channel_id=1, source_target_pairs={{0,1},{1,0},{2,3},{3,2},{4,5},{5,4},{6,7},{7,6},{8,9},{9,8},{10,11... | collective-permute-start | bytes 3981320 | tf_op jit(solution)/shard_map/ppermute | solution.py:460
  73.7 8.0 %collective-permute-start.9 = (bf16[640,512]{1,0:T(8,128)(2,1)S(1)}, bf16[640,512]{1,0:T(8,128)(2,1)S(1)}, u32[]{:S(2)}, u32[]{:S(2)}) collective-permute-start(bf16[640,512]{1,0:T(8,128)(2,1)S(1)} %collective-permute-done.2.refs_16_), channel_id=1, source_target_pairs={{0,1},{1,0},{2,3},{3,2},{4,5},{5,4},{6,7},{7,6},{8,9},{9,8},{10,11... | collective-permute-start | bytes 1966088 | tf_op jit(solution)/shard_map/ppermute | solution.py:460
  81.7 17.7 %copy-start.1 = (bf16[2,1024,512]{2,1,0:T(8,128)(2,1)S(1)}, bf16[2,1024,512]{2,1,0:T(8,128)(2,1)}, u32[]{:S(2)}) copy-start(bf16[2,1024,512]{2,1,0:T(8,128)(2,1)} %param.9) | copy-start | bytes 6291460
  82.6 70.5 %all-to-all-start.1 = ((bf16[256,8,512]{2,1,0:T(8,128)(2,1)}), bf16[256,8,512]{2,1,0:T(8,128)(2,1)}, u32[]{:S(2)}, u32[]{:S(2)}) async-start(bf16[256,8,512]{2,1,0:T(8,128)(2,1)} %second_mix.1), calls=%async_computation.1 | async-start | bytes 4194304 | tf_op jit(solution)/shard_map/all_to_all | solution.py:482
  96.5 15.6 %collective-permute-start.15 = (bf16[320,512]{1,0:T(8,128)(2,1)S(1)}, bf16[320,512]{1,0:T(8,128)(2,1)}, u32[]{:S(2)}, u32[]{:S(2)}) collective-permute-start(bf16[320,512]{1,0:T(8,128)(2,1)S(1)} %slice.13), channel_id=1, source_target_pairs={{0,64},{1,65},{2,66},{3,67},{4,68},{5,69},{6,70},{7,71},{8,72},{9,... | collective-permute-start | bytes 983048 | tf_op jit(solution)/shard_map/ppermute | solution.py:459
  98.0 17.8 %collective-permute-start.16 = (bf16[336,512]{1,0:T(8,128)(2,1)S(1)}, bf16[336,512]{1,0:T(8,128)(2,1)}, u32[]{:S(2)}, u32[]{:S(2)}) collective-permute-start(bf16[336,512]{1,0:T(8,128)(2,1)S(1)} %slice.14), channel_id=1, source_target_pairs={{0,192},{1,193},{2,194},{3,195},{4,196},{5,197},{6,198},{7,199},{8... | collective-permute-start | bytes 1032200 | tf_op jit(solution)/shard_map/ppermute | solution.py:459
  99.4 46.6 %copy-start.7 = (bf16[656,512]{1,0:T(8,128)(2,1)S(1)}, bf16[656,512]{1,0:T(8,128)(2,1)}, u32[]{:S(2)}) copy-start(bf16[656,512]{1,0:T(8,128)(2,1)} %copy-done.6) | copy-start | bytes 2015236
  100.4 24.2 %collective-permute-start.12 = (bf16[2,256,512]{2,1,0:T(8,128)(2,1)S(1)}, bf16[2,256,512]{2,1,0:T(8,128)(2,1)S(1)}, u32[]{:S(2)}, u32[]{:S(2)}) collective-permute-start(bf16[2,256,512]{2,1,0:T(8,128)(2,1)S(1)} %get-tuple-element.91), channel_id=1, source_target_pairs={{0,3},{1,2},{2,1},{3,0},{4,7},{5,6},{6,5},{7,4},{8,11},{9,10},{10,... | collective-permute-start | bytes 1572872 | tf_op jit(solution)/shard_map/ppermute | solution.py:459
  104.1 40.9 %collective-permute-start.14 = (bf16[640,512]{1,0:T(8,128)(2,1)S(1)}, bf16[640,512]{1,0:T(8,128)(2,1)S(1)}, u32[]{:S(2)}, u32[]{:S(2)}) collective-permute-start(bf16[640,512]{1,0:T(8,128)(2,1)S(1)} %copy-done.12), channel_id=1, source_target_pairs={{0,192},{1,193},{2,194},{3,195},{4,196},{5,197},{6,198},{7,199},{8... | collective-permute-start | bytes 1966088 | tf_op jit(solution)/shard_map/ppermute | solution.py:459
  105.4 39.7 %collective-permute-start.13 = (bf16[640,512]{1,0:T(8,128)(2,1)S(1)}, bf16[640,512]{1,0:T(8,128)(2,1)S(1)}, u32[]{:S(2)}, u32[]{:S(2)}) collective-permute-start(bf16[640,512]{1,0:T(8,128)(2,1)S(1)} %copy-done.12), channel_id=1, source_target_pairs={{0,64},{1,65},{2,66},{3,67},{4,68},{5,69},{6,70},{7,71},{8,72},{9,... | collective-permute-start | bytes 1966088 | tf_op jit(solution)/shard_map/ppermute | solution.py:459
  112.1 32.9 %collective-permute-start.11 = (bf16[2,256,512]{2,1,0:T(8,128)(2,1)S(1)}, bf16[2,256,512]{2,1,0:T(8,128)(2,1)S(1)}, u32[]{:S(2)}, u32[]{:S(2)}) collective-permute-start(bf16[2,256,512]{2,1,0:T(8,128)(2,1)S(1)} %get-tuple-element.92), channel_id=1, source_target_pairs={{0,2},{1,3},{2,0},{3,1},{4,6},{5,7},{6,4},{7,5},{8,10},{9,11},{10,... | collective-permute-start | bytes 1572872 | tf_op jit(solution)/shard_map/ppermute | solution.py:459
  115.8 29.2 %collective-permute-start.10 = (bf16[2,256,512]{2,1,0:T(8,128)(2,1)S(1)}, bf16[2,256,512]{2,1,0:T(8,128)(2,1)S(1)}, u32[]{:S(2)}, u32[]{:S(2)}) collective-permute-start(bf16[2,256,512]{2,1,0:T(8,128)(2,1)S(1)} %get-tuple-element.93), channel_id=1, source_target_pairs={{0,1},{1,0},{2,3},{3,2},{4,5},{5,4},{6,7},{7,6},{8,9},{9,8},{10,11... | collective-permute-start | bytes 1572872 | tf_op jit(solution)/shard_map/ppermute | solution.py:459
  124.6 20.5 %copy-start.20 = (bf16[2,256,512]{2,1,0:T(8,128)(2,1)}, bf16[2,256,512]{2,1,0:T(8,128)(2,1)S(1)}, u32[]{:S(2)}) copy-start(bf16[2,256,512]{2,1,0:T(8,128)(2,1)S(1)} %collective-permute-done.12.x3) | copy-start | bytes 1572868
  124.6 22.0 %collective-permute-start.22 = (bf16[640,512]{1,0:T(8,128)(2,1)S(1)}, bf16[640,512]{1,0:T(8,128)(2,1)S(1)}, u32[]{:S(2)}, u32[]{:S(2)}) collective-permute-start(bf16[640,512]{1,0:T(8,128)(2,1)S(1)} %copy-done.12), channel_id=1, source_target_pairs={{0,1},{1,0},{2,3},{3,2},{4,5},{5,4},{6,7},{7,6},{8,9},{9,8},{10,11... | collective-permute-start | bytes 1966088 | tf_op jit(solution)/shard_map/ppermute | solution.py:460
  145.1 2.9 %collective-permute-start.21 = (bf16[336,512]{1,0:T(8,128)(2,1)}, bf16[336,512]{1,0:T(8,128)(2,1)}, u32[]{:S(2)}, u32[]{:S(2)}) collective-permute-start(bf16[336,512]{1,0:T(8,128)(2,1)} %collective-permute-done.16.refs_12_), channel_id=1, source_target_pairs={{0,1},{1,0},{2,3},{3,2},{4,5},{5,4},{6,7},{7,6},{8,9},{9,8},{10,11... | collective-permute-start | bytes 1032200 | tf_op jit(solution)/shard_map/ppermute | solution.py:460
  145.8 2.0 %collective-permute-start.20 = (bf16[320,512]{1,0:T(8,128)(2,1)}, bf16[320,512]{1,0:T(8,128)(2,1)}, u32[]{:S(2)}, u32[]{:S(2)}) collective-permute-start(bf16[320,512]{1,0:T(8,128)(2,1)} %collective-permute-done.15.refs_11_), channel_id=1, source_target_pairs={{0,1},{1,0},{2,3},{3,2},{4,5},{5,4},{6,7},{7,6},{8,9},{9,8},{10,11... | collective-permute-start | bytes 983048 | tf_op jit(solution)/shard_map/ppermute | solution.py:460
  146.0 6.2 %collective-permute-start.17 = (bf16[656,512]{1,0:T(8,128)(2,1)S(1)}, bf16[656,512]{1,0:T(8,128)(2,1)S(1)}, u32[]{:S(2)}, u32[]{:S(2)}) collective-permute-start(bf16[656,512]{1,0:T(8,128)(2,1)S(1)} %copy-done.7), channel_id=1, source_target_pairs={{0,1},{1,0},{2,3},{3,2},{4,5},{5,4},{6,7},{7,6},{8,9},{9,8},{10,11... | collective-permute-start | bytes 2015240 | tf_op jit(solution)/shard_map/ppermute | solution.py:460
  146.3 5.9 %collective-permute-start.18 = (bf16[656,512]{1,0:T(8,128)(2,1)}, bf16[656,512]{1,0:T(8,128)(2,1)S(1)}, u32[]{:S(2)}, u32[]{:S(2)}) collective-permute-start(bf16[656,512]{1,0:T(8,128)(2,1)} %collective-permute-done.3.refs_9_), channel_id=1, source_target_pairs={{0,1},{1,0},{2,3},{3,2},{4,5},{5,4},{6,7},{7,6},{8,9},{9,8},{10,11... | collective-permute-start | bytes 2015240 | tf_op jit(solution)/shard_map/ppermute | solution.py:460
  146.7 6.4 %collective-permute-start.19 = (bf16[656,512]{1,0:T(8,128)(2,1)S(1)}, bf16[656,512]{1,0:T(8,128)(2,1)S(1)}, u32[]{:S(2)}, u32[]{:S(2)}) collective-permute-start(bf16[656,512]{1,0:T(8,128)(2,1)S(1)} %collective-permute-done.4.refs_10_), channel_id=1, source_target_pairs={{0,1},{1,0},{2,3},{3,2},{4,5},{5,4},{6,7},{7,6},{8,9},{9,8},{10,11... | collective-permute-start | bytes 2015240 | tf_op jit(solution)/shard_map/ppermute | solution.py:460
  147.8 3.5 %collective-permute-start.23 = (bf16[640,512]{1,0:T(8,128)(2,1)S(1)}, bf16[640,512]{1,0:T(8,128)(2,1)S(1)}, u32[]{:S(2)}, u32[]{:S(2)}) collective-permute-start(bf16[640,512]{1,0:T(8,128)(2,1)S(1)} %collective-permute-done.13.refs_14_), channel_id=1, source_target_pairs={{0,1},{1,0},{2,3},{3,2},{4,5},{5,4},{6,7},{7,6},{8,9},{9,8},{10,11... | collective-permute-start | bytes 1966088 | tf_op jit(solution)/shard_map/ppermute | solution.py:460
  147.9 4.3 %collective-permute-start.24 = (bf16[640,512]{1,0:T(8,128)(2,1)S(1)}, bf16[640,512]{1,0:T(8,128)(2,1)S(1)}, u32[]{:S(2)}, u32[]{:S(2)}) collective-permute-start(bf16[640,512]{1,0:T(8,128)(2,1)S(1)} %collective-permute-done.14.refs_15_), channel_id=1, source_target_pairs={{0,1},{1,0},{2,3},{3,2},{4,5},{5,4},{6,7},{7,6},{8,9},{9,8},{10,11... | collective-permute-start | bytes 1966088 | tf_op jit(solution)/shard_map/ppermute | solution.py:460
  (18 other events, 95.9 us)
